TPU v7x, 32 devices: a whole 2x2x4 slice. The times are simulated.
32 devices in a mesh: grp: 2 (over x), row: 4 (over y, core), col: 4 (over z).
Axes of the slice: x: 2, y: 2, z: 4, core: 2. Of those that a mesh axis runs over, the one named last changes fastest.
Arguments:
- phase: bfloat16 [64, 2, 128, 2048], P('grp', None, 'row', 'col'), may hold values from -6 to 6
- pseudo_inverse: bfloat16 [48, 64], replicated, may hold values from -0.75 to 0.75
- rotation: float32 [4, 3], replicated, may hold values from -4 to 4
- plate_id: int32 [256, 2048], P(('grp', 'row'), 'col'), may hold values from 0 to 3
- coherent: int32 [256, 2048], P(('grp', 'row'), 'col'), may hold values 0 or 1
Outputs:
- displacement: bfloat16 [48, 256, 2048], P(None, ('grp', 'row'), 'col')
- grad_rows: float32 [256, 2048], P(('grp', 'row'), 'col')
- grad_cols: float32 [256, 2048], P(('grp', 'row'), 'col')
All inputs are finite; a program needn't handle non-finite values. No bound on the sum of `coherent` on one device may be relied on, other than what follows from the above.
Results may differ from a plain program's by a relative error of at most 0.001.
Values may be sent and summed in bfloat16 or wider, within the bound.
A program may use at most 128 MiB of HBM per device.

v0:
```python
import jax
import jax.numpy as jnp
from jax import lax
from jax.sharding import PartitionSpec as P


def extended(block, sides, width):
    for axis, dim in sides:
        count = lax.axis_size(axis)
        forward = [(i, i + 1) for i in range(count - 1)]
        backward = [(target, source) for source, target in forward]
        low = lax.ppermute(
            lax.slice_in_dim(block, block.shape[dim] - width, None, axis=dim), axis, forward
        )
        high = lax.ppermute(lax.slice_in_dim(block, 0, width, axis=dim), axis, backward)
        block = jnp.concatenate([low, block, high], axis=dim)
    return block


def lever_field(rows, cols, total_rows, total_cols):
    lat = jnp.deg2rad(36.0 + 6.0 * (rows + 0.5) / total_rows)
    lon = jnp.deg2rad(26.0 + 19.0 * (cols + 0.5) / total_cols)
    px = jnp.cos(lat) * jnp.cos(lon)
    py = jnp.cos(lat) * jnp.sin(lon)
    pz = jnp.sin(lat) + 0.0 * lon
    sx, sy, sz = (0.38, -0.08, 0.92)
    return jnp.stack([py * sz - pz * sy, pz * sx - px * sz, px * sy - py * sx])


def on_device(phase, pseudo_inverse, rotation, plate_id, coherent):
    local_ifg = phase.shape[0]
    groups = phase.shape[1]
    tile_rows = plate_id.shape[0]
    tile_cols = plate_id.shape[1]
    epochs = pseudo_inverse.shape[0]
    own_cols = lax.dynamic_slice_in_dim(
        pseudo_inverse, lax.axis_index("grp") * local_ifg, local_ifg, 1
    )
    flat = phase.reshape(local_ifg, groups * tile_rows, tile_cols)
    summed = lax.psum_scatter(
        jnp.einsum("ei,irx->rex", own_cols, flat, preferred_element_type=jnp.float32),
        "grp",
        scatter_dimension=0,
        tiled=True,
    )
    series = jnp.transpose(summed, (1, 0, 2))
    displacement = series.astype(jnp.bfloat16)
    steps = jnp.arange(epochs, dtype=jnp.float32) - (epochs - 1) / 2.0
    slope = steps / jnp.sqrt(jnp.sum(steps * steps))
    rate = jnp.einsum("e,eyx->yx", slope, series, precision=lax.Precision.HIGHEST)
    tile_index = lax.axis_index("grp") * lax.axis_size("row") + lax.axis_index("row")
    total_rows = tile_rows * lax.axis_size("grp") * lax.axis_size("row")
    total_cols = tile_cols * lax.axis_size("col")
    rows = (tile_index * tile_rows).astype(jnp.float32) + jnp.arange(tile_rows, dtype=jnp.float32)[
        :, None
    ]
    cols = (lax.axis_index("col") * tile_cols).astype(jnp.float32) + jnp.arange(
        tile_cols, dtype=jnp.float32
    )[None, :]
    lever = lever_field(rows, cols, total_rows, total_cols)
    along = jnp.einsum("pk,kyx->pyx", rotation, lever, precision=lax.Precision.HIGHEST)
    plate_range = jnp.arange(rotation.shape[0], dtype=jnp.int32)[:, None, None]
    plate_rate = jnp.sum(jnp.where(plate_id[None] == plate_range, along, 0.0), axis=0)
    velocity = coherent.astype(jnp.float32) * rate - plate_rate
    reach = 16
    norm = jnp.sqrt(jnp.float32(reach * (reach + 1) * (2 * reach + 1) // 3))
    upright = extended(velocity, ((("grp", "row"), 0),), reach)
    sideways = extended(velocity, (("col", 1),), reach)
    grad_rows = jnp.zeros((tile_rows, tile_cols), jnp.float32)
    grad_cols = jnp.zeros((tile_rows, tile_cols), jnp.float32)
    for k in range(-reach, reach + 1):
        tap = k / norm
        grad_rows = grad_rows + tap * upright[reach + k : reach + k + tile_rows, :]
        grad_cols = grad_cols + tap * sideways[:, reach + k : reach + k + tile_cols]
    return (displacement, grad_rows, grad_cols)


def solution(mesh):
    return jax.shard_map(
        on_device,
        mesh=mesh,
        in_specs=(
            P("grp", None, "row", "col"),
            P(),
            P(),
            P(("grp", "row"), "col"),
            P(("grp", "row"), "col"),
        ),
        out_specs=(
            P(None, ("grp", "row"), "col"),
            P(("grp", "row"), "col"),
            P(("grp", "row"), "col"),
        ),
        check_vma=False,
    )
```

profile of v0, /device:TPU:0, one launch (start us, length us, event | category | flops | bytes accessed | tf_op | source)
XLA Modules:
  0.0 118.2 jit_solution(4388014009330853112)
XLA Ops:
  7.2 0.0 copy-start
  7.2 0.0 reduce-scatter.2.cloned.1.call-start
  7.2 1.5 %copy-done = bf16[32,2,32,512]{3,2,1,0:T(8,128)(2,1)S(1)} copy-done((bf16[32,2,32,512]{3,2,1,0:T(8,128)(2,1)S(1)}, bf16[32,2,32,512]{3,2,1,0:T(8,128)(2,1)}, u32[]{:S(2)}) %copy-start) | copy-done | bytes 2097176
  8.8 5.1 %convolution_bitcast_fusion = f32[64,48,512]{2,1,0:T(8,128)} fusion(bf16[32,64,512]{2,1,0:T(8,128)(2,1)S(1)} %bitcast.27, bf16[48,64]{1,0:T(8,128)(2,1)} %param.6, s32[]{:T(128)S(6)} %select_n.7), kind=kOutput, calls=%fused_computation.3 | convolution fusion | flops 100663296 | bytes 8394756 | tf_op jit(solution)/shard_map/ei,irx->rex/dot_general | solution.py:41
  13.8 0.0 copy-start.3
  13.8 0.0 copy-start.4
  13.8 0.0 reduce-scatter.2.cloned.1.call-update
  13.9 0.6 multiply_reduce_fusion
  15.2 0.1 fusion.207
  15.2 0.1 fusion.204
  15.3 0.1 fusion.201
  15.3 0.1 fusion.6
  15.4 0.0 copy-start.2
  15.5 0.0 copy-done.3
  15.5 0.0 copy-done.4
  15.5 0.8 fusion.4
  16.3 77.5 %reduce-scatter.2.cloned.1.call-done = f32[32,48,512]{2,1,0:T(8,128)} async-done(((f32[64,48,512]{2,1,0:T(8,128)}), f32[32,48,512]{2,1,0:T(8,128)}) %reduce-scatter.2.cloned.1.call-update) | async-done | bytes 3145744 | tf_op jit(solution)/shard_map/reduce_scatter | solution.py:40
  93.8 0.0 copy-start.1
  93.8 3.6 %fusion = f32[1,32,512]{2,0,1:T(1,128)S(1)} fusion(f32[32,48,512]{2,1,0:T(8,128)} %reduce-scatter.2.cloned.1.call-done, f32[]{:T(128)S(6)} %sqrt.3), kind=kOutput, calls=%fused_computation | convolution fusion | flops 9437280 | bytes 3211268 | tf_op jit(solution)/shard_map/e,eyx->yx/dot_general | solution.py:50
  97.4 0.0 copy-done.2
  97.4 0.1 fusion.213
  97.5 1.3 %collective-permute-start.3 = (f32[32,16]{1,0:T(8,128)S(1)}, f32[32,16]{1,0:T(8,128)S(1)}, u32[]{:S(2)}, u32[]{:S(2)}) collective-permute-start(f32[32,16]{1,0:T(8,128)S(1)} %get-tuple-element.12), channel_id=1, source_target_pairs={{1,0},{2,1},{3,2},{5,4},{6,5},{7,6},{9,8},{10,9},{11,10},{13,12},{... | collective-permute-start | bytes 6152 | tf_op jit(solution)/shard_map/ppermute | solution.py:15
  98.8 4.5 %collective-permute-start.2 = (f32[32,16]{1,0:T(8,128)S(1)}, f32[32,16]{1,0:T(8,128)S(1)}, u32[]{:S(2)}, u32[]{:S(2)}) collective-permute-start(f32[32,16]{1,0:T(8,128)S(1)} %get-tuple-element.11), channel_id=1, source_target_pairs={{0,1},{1,2},{2,3},{4,5},{5,6},{6,7},{8,9},{9,10},{10,11},{12,13},{... | collective-permute-start | bytes 6152 | tf_op jit(solution)/shard_map/ppermute | solution.py:12
  103.3 1.3 %collective-permute-start.1 = (f32[16,512]{1,0:T(8,128)S(1)}, f32[16,512]{1,0:T(8,128)S(1)}, u32[]{:S(2)}, u32[]{:S(2)}) collective-permute-start(f32[16,512]{1,0:T(8,128)S(1)} %get-tuple-element.14), channel_id=1, source_target_pairs={{4,0},{8,4},{12,8},{16,12},{20,16},{24,20},{28,24},{5,1},{9,5},{13... | collective-permute-start | bytes 98312 | tf_op jit(solution)/shard_map/ppermute | solution.py:15
  104.6 3.0 %collective-permute-start = (f32[16,512]{1,0:T(8,128)S(1)}, f32[16,512]{1,0:T(8,128)S(1)}, u32[]{:S(2)}, u32[]{:S(2)}) collective-permute-start(f32[16,512]{1,0:T(8,128)S(1)} %get-tuple-element.13), channel_id=1, source_target_pairs={{0,4},{4,8},{8,12},{12,16},{16,20},{20,24},{24,28},{1,5},{5,9},{9,... | collective-permute-start | bytes 98312 | tf_op jit(solution)/shard_map/ppermute | solution.py:12
  107.7 0.0 copy-done.1
  107.7 0.2 bitcast_convert_fusion
  107.9 2.0 %copy.14 = bf16[48,32,512]{2,1,0:T(8,128)(2,1)} copy(bf16[48,32,512]{2,0,1:T(8,128)(2,1)S(1)} %bitcast_convert_fusion) | data formatting | bytes 3145728
  110.0 0.0 collective-permute-done.3
  110.0 0.0 collective-permute-done.2
  110.0 0.0 collective-permute-done.1
  110.0 0.0 collective-permute-done
  110.0 1.4 %fusion.12 = (f32[32,512]{1,0:T(8,128)}, f32[32,512]{1,0:T(8,128)}) fusion(f32[32,512]{1,0:T(8,128)S(1)} %fusion.197, f32[32,16]{1,0:T(8,128)S(1)} %collective-permute-done.3, f32[32,16]{1,0:T(8,128)S(1)} %collective-permute-done.2, f32[16,512]{1,0:T(8,128)S(1)} %collective-permute-done.1, f32[16,512]{1,0:T(8,128)S(1)} %collective-permute-done), kind=kLoop, calls=%fused_computation.143 | loop fusion | flops 3162112 | bytes 266240 | tf_op jit(solution)/shard_map/add | solution.py:74
  (3 shorter events, 0.0 us)
Async XLA Ops:
  7.2 1.6 %copy-start = (bf16[32,2,32,512]{3,2,1,0:T(8,128)(2,1)S(1)}, bf16[32,2,32,512]{3,2,1,0:T(8,128)(2,1)}, u32[]{:S(2)}) copy-start(bf16[32,2,32,512]{3,2,1,0:T(8,128)(2,1)} %param.5) | copy-start | bytes 6291460
  7.2 86.6 %reduce-scatter.2.cloned.1.call-start = ((), (), s32[]{:S(2)}) async-start(), calls=%async_computation.1 | async-start | bytes 9437184 | tf_op jit(solution)/shard_map/reduce_scatter | solution.py:40
  13.8 1.6 %copy-start.3 = (s32[32,512]{1,0:T(8,128)S(1)}, s32[32,512]{1,0:T(8,128)}, u32[]{:S(2)}) copy-start(s32[32,512]{1,0:T(8,128)} %param.8) | copy-start | bytes 196612
  13.8 1.7 %copy-start.4 = (f32[4,3]{1,0:T(4,128)S(1)}, f32[4,3]{1,0:T(4,128)}, u32[]{:S(2)}) copy-start(f32[4,3]{1,0:T(4,128)} %param.7) | copy-start | bytes 148
  15.4 81.9 %copy-start.2 = (s32[32,512]{1,0:T(8,128)S(1)}, s32[32,512]{1,0:T(8,128)}, u32[]{:S(2)}) copy-start(s32[32,512]{1,0:T(8,128)} %param.9) | copy-start | bytes 196612
  93.8 13.9 %copy-start.1 = (f32[32,48,512]{2,1,0:T(8,128)S(1)}, f32[32,48,512]{2,1,0:T(8,128)}, u32[]{:S(2)}) copy-start(f32[32,48,512]{2,1,0:T(8,128)} %reduce-scatter.2.cloned.1.call-done) | copy-start | bytes 9437188
  97.5 12.5 %collective-permute-start.3 = (f32[32,16]{1,0:T(8,128)S(1)}, f32[32,16]{1,0:T(8,128)S(1)}, u32[]{:S(2)}, u32[]{:S(2)}) collective-permute-start(f32[32,16]{1,0:T(8,128)S(1)} %get-tuple-element.12), channel_id=1, source_target_pairs={{1,0},{2,1},{3,2},{5,4},{6,5},{7,6},{9,8},{10,9},{11,10},{13,12},{... | collective-permute-start | bytes 6152 | tf_op jit(solution)/shard_map/ppermute | solution.py:15
  98.8 11.2 %collective-permute-start.2 = (f32[32,16]{1,0:T(8,128)S(1)}, f32[32,16]{1,0:T(8,128)S(1)}, u32[]{:S(2)}, u32[]{:S(2)}) collective-permute-start(f32[32,16]{1,0:T(8,128)S(1)} %get-tuple-element.11), channel_id=1, source_target_pairs={{0,1},{1,2},{2,3},{4,5},{5,6},{6,7},{8,9},{9,10},{10,11},{12,13},{... | collective-permute-start | bytes 6152 | tf_op jit(solution)/shard_map/ppermute | solution.py:12
  103.3 6.6 %collective-permute-start.1 = (f32[16,512]{1,0:T(8,128)S(1)}, f32[16,512]{1,0:T(8,128)S(1)}, u32[]{:S(2)}, u32[]{:S(2)}) collective-permute-start(f32[16,512]{1,0:T(8,128)S(1)} %get-tuple-element.14), channel_id=1, source_target_pairs={{4,0},{8,4},{12,8},{16,12},{20,16},{24,20},{28,24},{5,1},{9,5},{13... | collective-permute-start | bytes 98312 | tf_op jit(solution)/shard_map/ppermute | solution.py:15
  104.6 5.3 %collective-permute-start = (f32[16,512]{1,0:T(8,128)S(1)}, f32[16,512]{1,0:T(8,128)S(1)}, u32[]{:S(2)}, u32[]{:S(2)}) collective-permute-start(f32[16,512]{1,0:T(8,128)S(1)} %get-tuple-element.13), channel_id=1, source_target_pairs={{0,4},{4,8},{8,12},{12,16},{16,20},{20,24},{24,28},{1,5},{5,9},{9,... | collective-permute-start | bytes 98312 | tf_op jit(solution)/shard_map/ppermute | solution.py:12
Sparse Core Ops, SparseCore 0:
  14.0 79.7 reduce-scatter.1
where the time goes:
time: 119 us; the launch traced here: 118 us
  waiting for transfers between devices  77.5 us (65%)
  between operations  14.9 us (13%)
  starting transfers between devices  10.2 us (9%)
  matrix products  9.49 us (8%)
  local copies, waits for them, and re-layouts  3.64 us (3%)
  other arithmetic  2.53 us (2%)
    reduce_scatter x1, waiting for transfers between devices, on_device(): lax.psum_scatter(jnp.einsum('ei,irx->rex', own_cols, flat, preferred_elem...  77.5 us
    ppermute x2, starting transfers between devices, extended(): lax.ppermute(lax.slice_in_dim(block, block.shape[dim] - width, None, axis...  7.58 us
    dot_general x1, matrix products, on_device(): jnp.einsum('ei,irx->rex', own_cols, flat, preferred_element_type=jnp.floa...  5.06 us
    dot_general x1, matrix products, on_device(): jnp.einsum('e,eyx->yx', slope, series, precision=lax.Precision.HIGHEST)  3.62 us
    unnamed x11, local copies, waits for them, and re-layouts  3.56 us
    ppermute x2, starting transfers between devices, extended(): lax.ppermute(lax.slice_in_dim(block, 0, width, axis=dim), axis, backward)  2.57 us
  transfers between devices with their start and end apart: 5, of which 1 were waited for; matrix products, arithmetic and copies ran while one was open for 3% of the time, Pallas kernels for 0%

commit v1 on v0

v1 whole, which is shorter than its diff:
```python
import functools

import jax
import jax.numpy as jnp
from jax import lax
from jax.experimental import pallas as pl
from jax.experimental.pallas import tpu as pltpu
from jax.sharding import PartitionSpec as P

MESH = pl.DeviceIdType.MESH
REACH = 16
SUB = 16
SPLITS = 3
EARLY, MIDDLE = 2, 3


def iota(shape, dim):
    return lax.broadcasted_iota(jnp.int32, shape, dim)


def parts_of(value):
    high = value.astype(jnp.bfloat16)
    rest = value - high.astype(jnp.float32)
    middle = rest.astype(jnp.bfloat16)
    low = (rest - middle.astype(jnp.float32)).astype(jnp.bfloat16)
    return high, middle, low


def dot(a, b):
    return jnp.dot(a, b, preferred_element_type=jnp.float32)


def as_bf16(mask):
    return jnp.where(mask, 1.0, 0.0).astype(jnp.bfloat16)


def kernel(
    sizes, phase, inverse_hbm, rotation, plate_hbm, coherent_hbm,
    disp, grad_rows, grad_cols,
    stack, mine, inverse, plate, coherent, weights, partial, incoming, tall, wide,
    local_sem, bulk_send, bulk_recv, rate_send, rate_recv, halo_send, halo_recv,
):
    n_grp, n_row, n_col = sizes
    _, share, tile_rows, tile_cols = stack.shape
    epochs, ifgs = inverse.shape
    grp, row, col = lax.axis_index("grp"), lax.axis_index("row"), lax.axis_index("col")
    tile = grp * n_row + row
    tiles = n_grp * n_row

    locals_ = [
        pltpu.make_async_copy(inverse_hbm, inverse, local_sem.at[0]),
        pltpu.make_async_copy(plate_hbm, plate, local_sem.at[1]),
        pltpu.make_async_copy(coherent_hbm, coherent, local_sem.at[2]),
        pltpu.make_async_copy(phase.at[:, grp], stack.at[0], local_sem.at[3]),
    ]
    targets = [lax.rem(grp + s, n_grp) for s in range(n_grp)]
    for s in range(1, n_grp):
        locals_.append(
            pltpu.make_async_copy(phase.at[:, targets[s]], mine.at[s - 1], local_sem.at[3 + s])
        )
    for copy in locals_:
        copy.start()

    above, below = tile - 1, tile + 1
    places = [
        {"grp": lax.div(jnp.maximum(above, 0), n_row), "row": lax.rem(jnp.maximum(above, 0), n_row)},
        {"grp": lax.rem(lax.div(below, n_row), n_grp), "row": lax.rem(below, n_row)},
        {"col": jnp.maximum(col - 1, 0)},
        {"col": jnp.minimum(col + 1, n_col - 1)},
    ]
    there = [tile > 0, tile < tiles - 1, col > 0, col < n_col - 1]

    barrier = pltpu.get_barrier_semaphore()
    for s in range(1, n_grp):
        pl.semaphore_signal(barrier, inc=1, device_id={"grp": targets[s]}, device_id_type=MESH)
    for place, exists in zip(places, there):
        @pl.when(exists)
        def _(place=place):
            pl.semaphore_signal(barrier, inc=1, device_id=place, device_id_type=MESH)
    peers = n_grp - 1
    for exists in there:
        peers = peers + jnp.where(exists, 1, 0)
    pl.semaphore_wait(barrier, peers)

    half = tile_cols // 2
    chunks = [(y, x) for y in range(0, tile_rows, SUB) for x in range(0, tile_cols, half)]

    def bulk(s, c):
        y, x = chunks[c]
        return pltpu.make_async_remote_copy(
            src_ref=phase.at[:, targets[s], pl.ds(y, SUB), pl.ds(x, half)],
            dst_ref=stack.at[s, :, pl.ds(y, SUB), pl.ds(x, half)],
            send_sem=bulk_send.at[s - 1, c],
            recv_sem=bulk_recv.at[s - 1, c],
            device_id={"grp": targets[s]},
            device_id_type=MESH,
        )

    bulks = [[bulk(s, c) for s in range(1, n_grp)] for c in range(len(chunks))]
    for c in range(EARLY):
        for copy in bulks[c]:
            copy.start()

    locals_[0].wait()
    steps = iota((epochs, 1), 0).astype(jnp.float32) - (epochs - 1) / 2.0
    slope = steps / jnp.sqrt(jnp.sum(steps * steps, axis=0, keepdims=True))
    rate_weight = jnp.sum(inverse[...].astype(jnp.float32) * slope, axis=0, keepdims=True)
    high, middle, low = parts_of(rate_weight)
    pick = iota((SPLITS * SUB, ifgs), 0) // SUB
    spread = jnp.where(
        pick == 0,
        high.astype(jnp.float32),
        jnp.where(pick == 1, middle.astype(jnp.float32), low.astype(jnp.float32)),
    ).astype(jnp.bfloat16)
    depth = share * SUB
    own = as_bf16(iota((ifgs, depth), 0) == grp * share + iota((ifgs, depth), 1) // SUB)
    diagonal = (iota((SPLITS * SUB, depth), 0) & (SUB - 1)) == (
        iota((SPLITS * SUB, depth), 1) & (SUB - 1)
    )
    rate_matrix = jnp.where(diagonal, dot(spread, own), 0.0).astype(jnp.bfloat16)

    def partial_rate(block, slot):
        for y in range(0, tile_rows, SUB):
            data = block[:, pl.ds(y, SUB), :].reshape(depth, tile_cols)
            three = dot(rate_matrix, data)
            partial[slot, pl.ds(y, SUB), :] = (
                three[:SUB] + three[SUB:2 * SUB] + three[2 * SUB:]
            )

    rates = []
    for s in range(1, n_grp):
        locals_[3 + s].wait()
        partial_rate(mine.at[s - 1], s)
        rates.append(
            pltpu.make_async_remote_copy(
                src_ref=partial.at[s],
                dst_ref=incoming.at[s - 1],
                send_sem=rate_send.at[s - 1],
                recv_sem=rate_recv.at[s - 1],
                device_id={"grp": targets[s]},
                device_id_type=MESH,
            )
        )
        rates[-1].start()
    for c in range(EARLY, MIDDLE):
        for copy in bulks[c]:
            copy.start()
    locals_[3].wait()
    partial_rate(stack.at[0], 0)

    locals_[1].wait()
    locals_[2].wait()
    ys = (tile * tile_rows + iota((tile_rows, 128), 0)).astype(jnp.float32)
    xs = (col * tile_cols + iota((8, tile_cols), 1)).astype(jnp.float32)
    lat = jnp.deg2rad(36.0 + 6.0 * (ys + 0.5) / (tiles * tile_rows))
    lon = jnp.deg2rad(26.0 + 19.0 * (xs + 0.5) / (n_col * tile_cols))
    cos_lat, sin_lat = jnp.cos(lat)[:, :1], jnp.sin(lat)[:, :1]
    cos_lon, sin_lon = jnp.cos(lon)[:1], jnp.sin(lon)[:1]
    px, py = cos_lat * cos_lon, cos_lat * sin_lon
    pz = sin_lat + jnp.zeros_like(px)
    sx, sy, sz = (0.38, -0.08, 0.92)
    lever = (py * sz - pz * sy, pz * sx - px * sz, px * sy - py * sx)
    plate_rate = jnp.zeros((tile_rows, tile_cols), jnp.float32)
    for p in range(rotation.shape[0]):
        along = rotation[p, 0] * lever[0] + rotation[p, 1] * lever[1] + rotation[p, 2] * lever[2]
        plate_rate = jnp.where(plate[...] == p, along, plate_rate)

    rate = partial[0]
    for s in range(1, n_grp):
        rates[s - 1].wait_recv()
        rate = rate + incoming[s - 1]
    velocity = coherent[...].astype(jnp.float32) * rate - plate_rate
    tall[pl.ds(REACH, tile_rows), :] = velocity
    wide[:, pl.ds(128, tile_cols)] = velocity

    halo_from = [
        tall.at[pl.ds(REACH, REACH), :],
        tall.at[pl.ds(tile_rows, REACH), :],
        wide.at[:, pl.ds(128, 128)],
        wide.at[:, pl.ds(tile_cols, 128)],
    ]
    halo_to = [
        tall.at[pl.ds(REACH + tile_rows, REACH), :],
        tall.at[pl.ds(0, REACH), :],
        wide.at[:, pl.ds(128 + tile_cols, 128)],
        wide.at[:, pl.ds(0, 128)],
    ]
    opposite = [1, 0, 3, 2]
    halos = [
        pltpu.make_async_remote_copy(
            src_ref=halo_from[d],
            dst_ref=halo_to[d],
            send_sem=halo_send.at[d],
            recv_sem=halo_recv.at[d],
            device_id=places[d],
            device_id_type=MESH,
        )
        for d in range(4)
    ]
    for d in range(4):
        pl.when(there[d])(halos[d].start)
    for c in range(MIDDLE, len(chunks)):
        for copy in bulks[c]:
            copy.start()

    full = ifgs * SUB
    rows_of = as_bf16(iota((epochs * SUB, epochs), 0) // SUB == iota((epochs * SUB, epochs), 1))
    tall_inverse = dot(rows_of, inverse[...]).astype(jnp.bfloat16)
    for s in range(n_grp):
        source = lax.rem(grp + n_grp - s, n_grp)
        spot = as_bf16(iota((ifgs, depth), 0) == source * share + iota((ifgs, depth), 1) // SUB)
        same = (iota((epochs * SUB, depth), 0) & (SUB - 1)) == (
            iota((epochs * SUB, depth), 1) & (SUB - 1)
        )
        weights[:, pl.ds(s * depth, depth)] = jnp.where(same, dot(tall_inverse, spot), 0.0).astype(
            jnp.bfloat16
        )

    def series(c):
        y, x = chunks[c]
        for copy in bulks[c]:
            copy.wait_recv()
        data = stack[:, :, pl.ds(y, SUB), pl.ds(x, half)].reshape(full, half)
        out = dot(weights[...], data).reshape(epochs, SUB, half)
        disp[:, pl.ds(y, SUB), pl.ds(x, half)] = out.astype(jnp.bfloat16)

    for c in range(EARLY):
        series(c)

    for d in range(4):
        pl.when(there[d])(halos[d].wait_send)
        pl.when(there[opposite[d]])(halos[d].wait_recv)

        @pl.when(jnp.logical_not(there[opposite[d]]))
        def _(d=d):
            halo_to[d][...] = jnp.zeros(halo_to[d].shape, jnp.float32)
    scale = 1.0 / (float(REACH * (REACH + 1) * (2 * REACH + 1) // 3) ** 0.5)
    shape = (tile_rows, tile_rows + 2 * REACH)
    k = iota(shape, 1) - REACH - iota(shape, 0)
    taps = jnp.where(jnp.abs(k) <= REACH, k, 0).astype(jnp.float32).astype(jnp.bfloat16)
    total = None
    for part in parts_of(tall[...]):
        term = dot(taps, part)
        total = term if total is None else total + term
    grad_rows[...] = total * scale
    shape = (tile_cols + 256, tile_cols)
    k = iota(shape, 0) - 128 - iota(shape, 1)
    taps = jnp.where(jnp.abs(k) <= REACH, k, 0).astype(jnp.float32).astype(jnp.bfloat16)
    total = None
    for part in parts_of(wide[...]):
        term = dot(part, taps)
        total = term if total is None else total + term
    grad_cols[...] = total * scale

    for c in range(EARLY, len(chunks)):
        series(c)
    for c in range(len(chunks)):
        for copy in bulks[c]:
            copy.wait_send()
    for copy in rates:
        copy.wait_send()


def on_device(sizes, phase, pseudo_inverse, rotation, plate_id, coherent):
    share, n_grp, tile_rows, tile_cols = phase.shape
    epochs, ifgs = pseudo_inverse.shape
    anywhere = pl.BlockSpec(memory_space=pl.ANY)
    vmem = pl.BlockSpec(memory_space=pltpu.VMEM)
    f32, bf16 = jnp.float32, jnp.bfloat16
    others = n_grp - 1
    chunks = (tile_rows // SUB) * 2
    dma = pltpu.SemaphoreType.DMA
    return pl.pallas_call(
        functools.partial(kernel, sizes),
        out_shape=(
            jax.ShapeDtypeStruct((epochs, tile_rows, tile_cols), bf16),
            jax.ShapeDtypeStruct((tile_rows, tile_cols), f32),
            jax.ShapeDtypeStruct((tile_rows, tile_cols), f32),
        ),
        in_specs=[
            anywhere, anywhere, pl.BlockSpec(memory_space=pltpu.SMEM), anywhere, anywhere,
        ],
        out_specs=(vmem, vmem, vmem),
        scratch_shapes=[
            pltpu.VMEM((n_grp, share, tile_rows, tile_cols), bf16),
            pltpu.VMEM((others, share, tile_rows, tile_cols), bf16),
            pltpu.VMEM((epochs, ifgs), bf16),
            pltpu.VMEM((tile_rows, tile_cols), jnp.int32),
            pltpu.VMEM((tile_rows, tile_cols), jnp.int32),
            pltpu.VMEM((epochs * SUB, ifgs * SUB), bf16),
            pltpu.VMEM((n_grp, tile_rows, tile_cols), f32),
            pltpu.VMEM((others, tile_rows, tile_cols), f32),
            pltpu.VMEM((tile_rows + 2 * REACH, tile_cols), f32),
            pltpu.VMEM((tile_rows, tile_cols + 256), f32),
            dma((3 + n_grp,)),
            dma((others, chunks)),
            dma((others, chunks)),
            dma((others,)),
            dma((others,)),
            dma((4,)),
            dma((4,)),
        ],
        compiler_params=pltpu.CompilerParams(
            collective_id=0, has_side_effects=True, vmem_limit_bytes=48 * 1024 * 1024
        ),
        cost_estimate=pl.CostEstimate(
            flops=2 * epochs * ifgs * SUB * tile_rows * tile_cols,
            bytes_accessed=8 * 1024 * 1024,
            transcendentals=0,
        ),
    )(phase, pseudo_inverse, rotation, plate_id, coherent)


def solution(mesh):
    sizes = (mesh.shape["grp"], mesh.shape["row"], mesh.shape["col"])
    return jax.shard_map(
        functools.partial(on_device, sizes),
        mesh=mesh,
        in_specs=(
            P("grp", None, "row", "col"),
            P(),
            P(),
            P(("grp", "row"), "col"),
            P(("grp", "row"), "col"),
        ),
        out_specs=(
            P(None, ("grp", "row"), "col"),
            P(("grp", "row"), "col"),
            P(("grp", "row"), "col"),
        ),
        check_vma=False,
    )
```

time: 119 us -> 39.8 us (0.33)
  waiting for transfers between devices: 77.5 us -> 0 us
  Pallas kernels: 0 us -> 31.8 us
  between operations: 14.9 us -> 0.65 us
  starting transfers between devices: 10.2 us -> 0 us
  matrix products: 9.49 us -> 0 us
  local copies, waits for them, and re-layouts: 3.64 us -> 7.05 us
  other arithmetic: 2.53 us -> 0 us
    reduce_scatter x1 -> x0, waiting for transfers between devices: 77.5 us -> none  [on_device(): lax.psum_scatter(jnp.einsum('ei,irx->rex', own_cols, flat, preferred_elem...]
    pallas_call x0 -> x1, Pallas kernels: none -> 31.8 us  [on_device(): pl.pallas_call(functools.partial(kernel, sizes), out_shape=(jax.ShapeDtyp...]
    ppermute x4 -> x0, starting transfers between devices: 10.2 us -> none  [the longest x2 7.58 us: extended(): lax.ppermute(lax.slice_in_dim(block, block.shape[dim] - width, None, axis...]
    dot_general x3 -> x0, matrix products: 9.49 us -> none  [the longest x1 5.06 us: on_device(): jnp.einsum('ei,irx->rex', own_cols, flat, preferred_element_type=jnp.floa...]
    unnamed x11 -> x13, local copies, waits for them, and re-layouts: 3.56 us -> 7.05 us
    add x1 -> x0, other arithmetic: 1.38 us -> none  [on_device(): grad_cols = grad_cols + tap * sideways[:, reach + k:reach + k + tile_cols]]
  transfers between devices with their start and end apart: 5 -> 0, of which waited for: 1 -> 0; matrix products, arithmetic and copies ran while one was open for 3% -> 0% of each run, Pallas kernels for 0% -> 0%
where the time goes in v1:
time: 39.8 us; the launch traced here: 39.5 us
  Pallas kernels  31.8 us (80%)
  local copies, waits for them, and re-layouts  7.05 us (18%)
  between operations  0.65 us (2%)
    pallas_call x1, Pallas kernels, on_device(): pl.pallas_call(functools.partial(kernel, sizes), out_shape=(jax.ShapeDtyp...  31.8 us
    unnamed x13, local copies, waits for them, and re-layouts  7.05 us

profile of v1, /device:TPU:0, one launch (start us, length us, event | category | flops | bytes accessed | tf_op | source)
XLA Modules:
  0.0 39.5 jit_solution(3841140646750031661)
XLA Ops:
  0.6 0.0 copy-start
  0.6 1.6 %copy-done = bf16[32,2,32,512]{3,2,1,0:T(8,128)(2,1)S(1)} copy-done((bf16[32,2,32,512]{3,2,1,0:T(8,128)(2,1)S(1)}, bf16[32,2,32,512]{3,2,1,0:T(8,128)(2,1)}, u32[]{:S(2)}) %copy-start) | copy-done | bytes 2097176
  2.2 0.0 copy-start.1
  2.2 0.8 %copy-done.1 = s32[32,512]{1,0:T(8,128)S(1)} copy-done((s32[32,512]{1,0:T(8,128)S(1)}, s32[32,512]{1,0:T(8,128)}, u32[]{:S(2)}) %copy-start.1) | copy-done | bytes 65560
  3.1 0.0 copy-start.2
  3.1 0.8 %copy-done.2 = s32[32,512]{1,0:T(8,128)S(1)} copy-done((s32[32,512]{1,0:T(8,128)S(1)}, s32[32,512]{1,0:T(8,128)}, u32[]{:S(2)}) %copy-start.2) | copy-done | bytes 65560
  3.9 0.0 copy-start.3
  3.9 0.7 %copy-done.3 = bf16[48,64]{1,0:T(8,128)(2,1)S(1)} copy-done((bf16[48,64]{1,0:T(8,128)(2,1)S(1)}, bf16[48,64]{1,0:T(8,128)(2,1)}, u32[]{:S(2)}) %copy-start.3) | copy-done | bytes 6168
  4.6 0.0 copy-start.4
  4.6 0.7 %copy-done.4 = f32[4,3]{1,0:T(4,128)S(1)} copy-done((f32[4,3]{1,0:T(4,128)S(1)}, f32[4,3]{1,0:T(4,128)}, u32[]{:S(2)}) %copy-start.4) | copy-done | bytes 72
  5.3 31.8 %shard_map.76 = (bf16[48,32,512]{2,1,0:T(8,128)(2,1)S(1)}, f32[32,512]{1,0:T(8,128)S(1)}, f32[32,512]{1,0:T(8,128)S(1)}) custom-call(bf16[32,2,32,512]{3,2,1,0:T(8,128)(2,1)S(1)} %copy-done, bf16[48,64]{1,0:T(8,128)(2,1)S(1)} %copy-done.3, f32[4,3]{1,0:T(4,128)S(1)} %copy-done.4, s32[32,512]{1,0:T(8,128)S(1)} %copy-done.1, s32[32,512]{1,0:T(8,128)S(1)} %copy-done.2), custom_call_target="tpu_custom_call" | custom-call | flops 1610612736 | bytes 8388608 | tf_op jit(solution)/shard_map/pallas_call | solution.py:273
  37.1 1.1 %copy.11 = bf16[48,32,512]{2,1,0:T(8,128)(2,1)} copy(bf16[48,32,512]{2,1,0:T(8,128)(2,1)S(1)} %get-tuple-element.6) | data formatting | bytes 3145728
  38.3 0.6 %copy.12 = f32[32,512]{1,0:T(8,128)} copy(f32[32,512]{1,0:T(8,128)S(1)} %get-tuple-element.7) | data formatting | bytes 131072
  38.9 0.6 %copy.13 = f32[32,512]{1,0:T(8,128)} copy(f32[32,512]{1,0:T(8,128)S(1)} %get-tuple-element.8) | data formatting | bytes 131072
Async XLA Ops:
  0.6 1.6 %copy-start = (bf16[32,2,32,512]{3,2,1,0:T(8,128)(2,1)S(1)}, bf16[32,2,32,512]{3,2,1,0:T(8,128)(2,1)}, u32[]{:S(2)}) copy-start(bf16[32,2,32,512]{3,2,1,0:T(8,128)(2,1)} %phase.1) | copy-start | bytes 6291460
  2.2 0.8 %copy-start.1 = (s32[32,512]{1,0:T(8,128)S(1)}, s32[32,512]{1,0:T(8,128)}, u32[]{:S(2)}) copy-start(s32[32,512]{1,0:T(8,128)} %plate_hbm.1) | copy-start | bytes 196612
  3.1 0.8 %copy-start.2 = (s32[32,512]{1,0:T(8,128)S(1)}, s32[32,512]{1,0:T(8,128)}, u32[]{:S(2)}) copy-start(s32[32,512]{1,0:T(8,128)} %coherent_hbm.1) | copy-start | bytes 196612
  3.9 0.7 %copy-start.3 = (bf16[48,64]{1,0:T(8,128)(2,1)S(1)}, bf16[48,64]{1,0:T(8,128)(2,1)}, u32[]{:S(2)}) copy-start(bf16[48,64]{1,0:T(8,128)(2,1)} %inverse_hbm.1) | copy-start | bytes 18436
  4.6 0.7 %copy-start.4 = (f32[4,3]{1,0:T(4,128)S(1)}, f32[4,3]{1,0:T(4,128)}, u32[]{:S(2)}) copy-start(f32[4,3]{1,0:T(4,128)} %rotation.1) | copy-start | bytes 148

commit v2 on v1

--- a/solution.py
+++ b/solution.py
@@ -11,6 +11,8 @@
 REACH = 16
 SUB = 16
 SPLITS = 3
+GRANT = 63 * 1024 * 1024
+PIECES = 8
 EARLY, MIDDLE = 2, 3
 
 
@@ -35,10 +37,10 @@
 
 
 def kernel(
-    sizes, phase, inverse_hbm, rotation, plate_hbm, coherent_hbm,
-    disp, grad_rows, grad_cols,
-    stack, mine, inverse, plate, coherent, weights, partial, incoming, tall, wide,
-    local_sem, bulk_send, bulk_recv, rate_send, rate_recv, halo_send, halo_recv,
+    sizes, phase, inverse_hbm, rotation_hbm, plate_hbm, coherent_hbm,
+    disp_hbm, grad_rows_hbm, grad_cols_hbm,
+    disp, grad_rows, grad_cols, stack, mine, inverse, rotation, plate, coherent, weights, partial, incoming, tall, wide,
+    local_sem, bulk_send, bulk_recv, rate_send, rate_recv, halo_send, halo_recv, out_sem,
 ):
     n_grp, n_row, n_col = sizes
     _, share, tile_rows, tile_cols = stack.shape
@@ -52,11 +54,12 @@
         pltpu.make_async_copy(plate_hbm, plate, local_sem.at[1]),
         pltpu.make_async_copy(coherent_hbm, coherent, local_sem.at[2]),
         pltpu.make_async_copy(phase.at[:, grp], stack.at[0], local_sem.at[3]),
+        pltpu.make_async_copy(rotation_hbm, rotation, local_sem.at[4]),
     ]
     targets = [lax.rem(grp + s, n_grp) for s in range(n_grp)]
     for s in range(1, n_grp):
         locals_.append(
-            pltpu.make_async_copy(phase.at[:, targets[s]], mine.at[s - 1], local_sem.at[3 + s])
+            pltpu.make_async_copy(phase.at[:, targets[s]], mine.at[s - 1], local_sem.at[4 + s])
         )
     for copy in locals_:
         copy.start()
@@ -129,7 +132,7 @@
 
     rates = []
     for s in range(1, n_grp):
-        locals_[3 + s].wait()
+        locals_[4 + s].wait()
         partial_rate(mine.at[s - 1], s)
         rates.append(
             pltpu.make_async_remote_copy(
@@ -150,6 +153,7 @@
 
     locals_[1].wait()
     locals_[2].wait()
+    locals_[4].wait()
     ys = (tile * tile_rows + iota((tile_rows, 128), 0)).astype(jnp.float32)
     xs = (col * tile_cols + iota((8, tile_cols), 1)).astype(jnp.float32)
     lat = jnp.deg2rad(36.0 + 6.0 * (ys + 0.5) / (tiles * tile_rows))
@@ -223,6 +227,16 @@
         data = stack[:, :, pl.ds(y, SUB), pl.ds(x, half)].reshape(full, half)
         out = dot(weights[...], data).reshape(epochs, SUB, half)
         disp[:, pl.ds(y, SUB), pl.ds(x, half)] = out.astype(jnp.bfloat16)
+        write(
+            disp.at[:, pl.ds(y, SUB), pl.ds(x, half)],
+            disp_hbm.at[:, pl.ds(y, SUB), pl.ds(x, half)],
+        )
+
+    writes = []
+
+    def write(source, target):
+        writes.append(pltpu.make_async_copy(source, target, out_sem.at[len(writes)]))
+        writes[-1].start()
 
     for c in range(EARLY):
         series(c)
@@ -251,6 +265,8 @@
         term = dot(part, taps)
         total = term if total is None else total + term
     grad_cols[...] = total * scale
+    write(grad_rows, grad_rows_hbm)
+    write(grad_cols, grad_cols_hbm)
 
     for c in range(EARLY, len(chunks)):
         series(c)
@@ -259,18 +275,34 @@
             copy.wait_send()
     for copy in rates:
         copy.wait_send()
+    for copy in writes:
+        copy.wait()
+
+
+def write_out(disp, grad_rows, grad_cols, disp_hbm, grad_rows_hbm, grad_cols_hbm, sem):
+    copies = [
+        pltpu.make_async_copy(grad_rows, grad_rows_hbm, sem.at[0]),
+        pltpu.make_async_copy(grad_cols, grad_cols_hbm, sem.at[1]),
+    ]
+    size = disp.shape[0] // PIECES
+    for i in range(PIECES):
+        rows = pl.ds(i * size, size)
+        copies.append(pltpu.make_async_copy(disp.at[rows], disp_hbm.at[rows], sem.at[2 + i]))
+    for copy in copies:
+        copy.start()
+    for copy in copies:
+        copy.wait()
 
 
 def on_device(sizes, phase, pseudo_inverse, rotation, plate_id, coherent):
     share, n_grp, tile_rows, tile_cols = phase.shape
     epochs, ifgs = pseudo_inverse.shape
-    anywhere = pl.BlockSpec(memory_space=pl.ANY)
-    vmem = pl.BlockSpec(memory_space=pltpu.VMEM)
+    hbm = pl.BlockSpec(memory_space=pltpu.HBM)
     f32, bf16 = jnp.float32, jnp.bfloat16
     others = n_grp - 1
     chunks = (tile_rows // SUB) * 2
     dma = pltpu.SemaphoreType.DMA
-    return pl.pallas_call(
+    results = pl.pallas_call(
         functools.partial(kernel, sizes),
         out_shape=(
             jax.ShapeDtypeStruct((epochs, tile_rows, tile_cols), bf16),
@@ -278,13 +310,17 @@
             jax.ShapeDtypeStruct((tile_rows, tile_cols), f32),
         ),
         in_specs=[
-            anywhere, anywhere, pl.BlockSpec(memory_space=pltpu.SMEM), anywhere, anywhere,
+            hbm, hbm, hbm, hbm, hbm,
         ],
-        out_specs=(vmem, vmem, vmem),
+        out_specs=(hbm, hbm, hbm),
         scratch_shapes=[
+            pltpu.VMEM((epochs, tile_rows, tile_cols), bf16),
+            pltpu.VMEM((tile_rows, tile_cols), f32),
+            pltpu.VMEM((tile_rows, tile_cols), f32),
             pltpu.VMEM((n_grp, share, tile_rows, tile_cols), bf16),
             pltpu.VMEM((others, share, tile_rows, tile_cols), bf16),
             pltpu.VMEM((epochs, ifgs), bf16),
+            pltpu.SMEM(rotation.shape, f32),
             pltpu.VMEM((tile_rows, tile_cols), jnp.int32),
             pltpu.VMEM((tile_rows, tile_cols), jnp.int32),
             pltpu.VMEM((epochs * SUB, ifgs * SUB), bf16),
@@ -292,16 +328,17 @@
             pltpu.VMEM((others, tile_rows, tile_cols), f32),
             pltpu.VMEM((tile_rows + 2 * REACH, tile_cols), f32),
             pltpu.VMEM((tile_rows, tile_cols + 256), f32),
-            dma((3 + n_grp,)),
+            dma((4 + n_grp,)),
             dma((others, chunks)),
             dma((others, chunks)),
             dma((others,)),
             dma((others,)),
             dma((4,)),
             dma((4,)),
+            dma((chunks + 2,)),
         ],
         compiler_params=pltpu.CompilerParams(
-            collective_id=0, has_side_effects=True, vmem_limit_bytes=48 * 1024 * 1024
+            collective_id=0, has_side_effects=True, vmem_limit_bytes=GRANT
         ),
         cost_estimate=pl.CostEstimate(
             flops=2 * epochs * ifgs * SUB * tile_rows * tile_cols,
@@ -309,6 +346,14 @@
             transcendentals=0,
         ),
     )(phase, pseudo_inverse, rotation, plate_id, coherent)
+    return pl.pallas_call(
+        write_out,
+        out_shape=tuple(jax.ShapeDtypeStruct(r.shape, r.dtype) for r in results),
+        in_specs=[hbm] * 3,
+        out_specs=(hbm,) * 3,
+        scratch_shapes=[dma((2 + PIECES,))],
+        compiler_params=pltpu.CompilerParams(vmem_limit_bytes=GRANT),
+    )(*results)
 
 
 def solution(mesh):

time: 39.8 us -> 85.5 us (2.15)
  Pallas kernels: 31.8 us -> 84.7 us
  local copies, waits for them, and re-layouts: 7.05 us -> 0 us
    pallas_call x0 -> x1, Pallas kernels: none -> 52.8 us  [on_device(): pl.pallas_call(write_out, out_shape=tuple((jax.ShapeDtypeStruct(r.shape,...]
    unnamed x13 -> x0, local copies, waits for them, and re-layouts: 7.05 us -> none
where the time goes in v2:
time: 85.5 us; the launch traced here: 85.4 us
  Pallas kernels  84.7 us (99%)
    pallas_call x1, Pallas kernels, on_device(): pl.pallas_call(write_out, out_shape=tuple((jax.ShapeDtypeStruct(r.shape,...  52.8 us
    pallas_call x1, Pallas kernels, on_device(): pl.pallas_call(functools.partial(kernel, sizes), out_shape=(jax.ShapeDtyp...  31.9 us

profile of v2, /device:TPU:0, one launch (start us, length us, event | category | flops | bytes accessed | tf_op | source)
XLA Modules:
  0.0 85.4 jit_solution(6296963865046164890)
XLA Ops:
  0.6 31.9 %shard_map.76 = (bf16[48,32,512]{2,1,0:T(8,128)(2,1)}, f32[32,512]{1,0:T(8,128)}, f32[32,512]{1,0:T(8,128)}) custom-call(bf16[32,2,32,512]{3,2,1,0:T(8,128)(2,1)} %phase.1, bf16[48,64]{1,0:T(8,128)(2,1)} %inverse_hbm.1, f32[4,3]{1,0:T(4,128)} %rotation_hbm.1, s32[32,512]{1,0:T(8,128)} %plate_hbm.1, s32[32,512]{1,0:T(8,128)} %coherent_hbm.1), custom_call_target="tpu_custom_call" | custom-call | flops 1610612736 | bytes 8388608 | tf_op jit(solution)/shard_map/pallas_call | solution.py:305
  32.6 52.8 %shard_map.77 = (bf16[48,32,512]{2,1,0:T(8,128)(2,1)}, f32[32,512]{1,0:T(8,128)}, f32[32,512]{1,0:T(8,128)}) custom-call(bf16[48,32,512]{2,1,0:T(8,128)(2,1)} %get-tuple-element.6.disp, f32[32,512]{1,0:T(8,128)} %get-tuple-element.7.grad_rows, f32[32,512]{1,0:T(8,128)} %get-tuple-element.8.grad_cols), custom_call_target="tpu_custom_call" | custom-call | tf_op jit(solution)/shard_map/pallas_call | solution.py:349

commit v3 on v2

--- a/solution.py
+++ b/solution.py
@@ -12,8 +12,8 @@
 SUB = 16
 SPLITS = 3
 GRANT = 63 * 1024 * 1024
-PIECES = 8
-EARLY, MIDDLE = 2, 3
+PIECES = 4
+EARLY, MIDDLE = 2, 4
 
 
 def iota(shape, dim):
@@ -279,19 +279,24 @@
         copy.wait()
 
 
-def write_out(disp, grad_rows, grad_cols, disp_hbm, grad_rows_hbm, grad_cols_hbm, sem):
-    copies = [
-        pltpu.make_async_copy(grad_rows, grad_rows_hbm, sem.at[0]),
-        pltpu.make_async_copy(grad_cols, grad_cols_hbm, sem.at[1]),
-    ]
+def write_out(disp, grad_rows, grad_cols, disp_hbm, grad_rows_hbm, grad_cols_hbm, *scratch):
+    held, held_rows, held_cols, in_sem, out_sem = scratch
     size = disp.shape[0] // PIECES
+    moves = []
     for i in range(PIECES):
-        rows = pl.ds(i * size, size)
-        copies.append(pltpu.make_async_copy(disp.at[rows], disp_hbm.at[rows], sem.at[2 + i]))
-    for copy in copies:
-        copy.start()
-    for copy in copies:
-        copy.wait()
+        part = pl.ds(i * size, size)
+        moves.append((disp.at[part], held.at[part], disp_hbm.at[part]))
+    moves.append((grad_rows, held_rows, grad_rows_hbm))
+    moves.append((grad_cols, held_cols, grad_cols_hbm))
+    reads = [pltpu.make_async_copy(a, b, in_sem.at[i]) for i, (a, b, c) in enumerate(moves)]
+    stores = [pltpu.make_async_copy(b, c, out_sem.at[i]) for i, (a, b, c) in enumerate(moves)]
+    for read in reads:
+        read.start()
+    for read, store in zip(reads, stores):
+        read.wait()
+        store.start()
+    for store in stores:
+        store.wait()
 
 
 def on_device(sizes, phase, pseudo_inverse, rotation, plate_id, coherent):
@@ -351,7 +356,8 @@
         out_shape=tuple(jax.ShapeDtypeStruct(r.shape, r.dtype) for r in results),
         in_specs=[hbm] * 3,
         out_specs=(hbm,) * 3,
-        scratch_shapes=[dma((2 + PIECES,))],
+        scratch_shapes=[pltpu.VMEM(r.shape, r.dtype) for r in results]
+        + [dma((PIECES + 2,)), dma((PIECES + 2,))],
         compiler_params=pltpu.CompilerParams(vmem_limit_bytes=GRANT),
     )(*results)
 

time: 85.5 us -> 35 us (0.41)
  Pallas kernels: 84.7 us -> 33.8 us
    pallas_call x1, Pallas kernels: 52.8 us -> 2.27 us  [on_device(): pl.pallas_call(write_out, out_shape=tuple((jax.ShapeDtypeStruct(r.shape,...]
where the time goes in v3:
time: 35 us; the launch traced here: 34.5 us
  Pallas kernels  33.8 us (97%)
  between operations  0.64 us (2%)
    pallas_call x1, Pallas kernels, on_device(): pl.pallas_call(functools.partial(kernel, sizes), out_shape=(jax.ShapeDtyp...  31.6 us
    pallas_call x1, Pallas kernels, on_device(): pl.pallas_call(write_out, out_shape=tuple((jax.ShapeDtypeStruct(r.shape,...  2.27 us

profile of v3, /device:TPU:0, one launch (start us, length us, event | category | flops | bytes accessed | tf_op | source)
XLA Modules:
  0.0 34.5 jit_solution(9669937053808452540)
XLA Ops:
  0.6 31.6 %shard_map.76 = (bf16[48,32,512]{2,1,0:T(8,128)(2,1)}, f32[32,512]{1,0:T(8,128)}, f32[32,512]{1,0:T(8,128)}) custom-call(bf16[32,2,32,512]{3,2,1,0:T(8,128)(2,1)} %phase.1, bf16[48,64]{1,0:T(8,128)(2,1)} %inverse_hbm.1, f32[4,3]{1,0:T(4,128)} %rotation_hbm.1, s32[32,512]{1,0:T(8,128)} %plate_hbm.1, s32[32,512]{1,0:T(8,128)} %coherent_hbm.1), custom_call_target="tpu_custom_call" | custom-call | flops 1610612736 | bytes 8388608 | tf_op jit(solution)/shard_map/pallas_call | solution.py:310
  32.2 2.3 %shard_map.77 = (bf16[48,32,512]{2,1,0:T(8,128)(2,1)}, f32[32,512]{1,0:T(8,128)}, f32[32,512]{1,0:T(8,128)}) custom-call(bf16[48,32,512]{2,1,0:T(8,128)(2,1)} %get-tuple-element.6.disp, f32[32,512]{1,0:T(8,128)} %get-tuple-element.7.grad_rows, f32[32,512]{1,0:T(8,128)} %get-tuple-element.8.grad_cols), custom_call_target="tpu_custom_call" | custom-call | tf_op jit(solution)/shard_map/pallas_call | solution.py:354

commit v4 on v3

--- a/solution.py
+++ b/solution.py
@@ -12,8 +12,8 @@
 SUB = 16
 SPLITS = 3
 GRANT = 63 * 1024 * 1024
-PIECES = 4
-EARLY, MIDDLE = 2, 4
+PIECES = 12
+EARLY, MIDDLE = 1, 3
 
 
 def iota(shape, dim):
@@ -34,6 +34,13 @@
 
 def as_bf16(mask):
     return jnp.where(mask, 1.0, 0.0).astype(jnp.bfloat16)
+
+
+def chunks_of(tile_rows, tile_cols):
+    half, quarter = tile_cols // 2, tile_cols // 4
+    chunks = [(y, x, half) for y in range(0, tile_rows, SUB) for x in (0, half)]
+    y, x, _ = chunks.pop()
+    return chunks + [(y, x, quarter), (y, x + quarter, quarter)]
 
 
 def kernel(
@@ -85,14 +92,13 @@
         peers = peers + jnp.where(exists, 1, 0)
     pl.semaphore_wait(barrier, peers)
 
-    half = tile_cols // 2
-    chunks = [(y, x) for y in range(0, tile_rows, SUB) for x in range(0, tile_cols, half)]
+    chunks = chunks_of(tile_rows, tile_cols)
 
     def bulk(s, c):
-        y, x = chunks[c]
+        y, x, width = chunks[c]
         return pltpu.make_async_remote_copy(
-            src_ref=phase.at[:, targets[s], pl.ds(y, SUB), pl.ds(x, half)],
-            dst_ref=stack.at[s, :, pl.ds(y, SUB), pl.ds(x, half)],
+            src_ref=phase.at[:, targets[s], pl.ds(y, SUB), pl.ds(x, width)],
+            dst_ref=stack.at[s, :, pl.ds(y, SUB), pl.ds(x, width)],
             send_sem=bulk_send.at[s - 1, c],
             recv_sem=bulk_recv.at[s - 1, c],
             device_id={"grp": targets[s]},
@@ -221,15 +227,15 @@
         )
 
     def series(c):
-        y, x = chunks[c]
+        y, x, width = chunks[c]
         for copy in bulks[c]:
             copy.wait_recv()
-        data = stack[:, :, pl.ds(y, SUB), pl.ds(x, half)].reshape(full, half)
-        out = dot(weights[...], data).reshape(epochs, SUB, half)
-        disp[:, pl.ds(y, SUB), pl.ds(x, half)] = out.astype(jnp.bfloat16)
+        data = stack[:, :, pl.ds(y, SUB), pl.ds(x, width)].reshape(full, width)
+        out = dot(weights[...], data).reshape(epochs, SUB, width)
+        disp[:, pl.ds(y, SUB), pl.ds(x, width)] = out.astype(jnp.bfloat16)
         write(
-            disp.at[:, pl.ds(y, SUB), pl.ds(x, half)],
-            disp_hbm.at[:, pl.ds(y, SUB), pl.ds(x, half)],
+            disp.at[:, pl.ds(y, SUB), pl.ds(x, width)],
+            disp_hbm.at[:, pl.ds(y, SUB), pl.ds(x, width)],
         )
 
     writes = []
@@ -305,7 +311,7 @@
     hbm = pl.BlockSpec(memory_space=pltpu.HBM)
     f32, bf16 = jnp.float32, jnp.bfloat16
     others = n_grp - 1
-    chunks = (tile_rows // SUB) * 2
+    chunks = len(chunks_of(tile_rows, tile_cols))
     dma = pltpu.SemaphoreType.DMA
     results = pl.pallas_call(
         functools.partial(kernel, sizes),

time: 35 us -> 35.1 us (level)
  Pallas kernels: 33.8 us -> 34.3 us
where the time goes in v4:
time: 35.1 us; the launch traced here: 34.9 us
  Pallas kernels  34.3 us (98%)
  between operations  0.64 us (2%)
    pallas_call x1, Pallas kernels, on_device(): pl.pallas_call(functools.partial(kernel, sizes), out_shape=(jax.ShapeDtyp...  31.9 us
    pallas_call x1, Pallas kernels, on_device(): pl.pallas_call(write_out, out_shape=tuple((jax.ShapeDtypeStruct(r.shape,...  2.4 us

profile of v4, /device:TPU:0, one launch (start us, length us, event | category | flops | bytes accessed | tf_op | source)
XLA Modules:
  0.0 34.9 jit_solution(2241310931591693077)
XLA Ops:
  0.6 31.9 %shard_map.76 = (bf16[48,32,512]{2,1,0:T(8,128)(2,1)}, f32[32,512]{1,0:T(8,128)}, f32[32,512]{1,0:T(8,128)}) custom-call(bf16[32,2,32,512]{3,2,1,0:T(8,128)(2,1)} %phase.1, bf16[48,64]{1,0:T(8,128)(2,1)} %inverse_hbm.1, f32[4,3]{1,0:T(4,128)} %rotation_hbm.1, s32[32,512]{1,0:T(8,128)} %plate_hbm.1, s32[32,512]{1,0:T(8,128)} %coherent_hbm.1), custom_call_target="tpu_custom_call" | custom-call | flops 1610612736 | bytes 8388608 | tf_op jit(solution)/shard_map/pallas_call | solution.py:316
  32.5 2.4 %shard_map.77 = (bf16[48,32,512]{2,1,0:T(8,128)(2,1)}, f32[32,512]{1,0:T(8,128)}, f32[32,512]{1,0:T(8,128)}) custom-call(bf16[48,32,512]{2,1,0:T(8,128)(2,1)} %get-tuple-element.6.disp, f32[32,512]{1,0:T(8,128)} %get-tuple-element.7.grad_rows, f32[32,512]{1,0:T(8,128)} %get-tuple-element.8.grad_cols), custom_call_target="tpu_custom_call" | custom-call | tf_op jit(solution)/shard_map/pallas_call | solution.py:360

commit v5 on v3

--- a/solution.py
+++ b/solution.py
@@ -12,8 +12,9 @@
 SUB = 16
 SPLITS = 3
 GRANT = 63 * 1024 * 1024
-PIECES = 4
-EARLY, MIDDLE = 2, 4
+PIECES = 12
+PARTS = 4
+EARLY, MIDDLE = 2, 6
 
 
 def iota(shape, dim):
@@ -34,6 +35,11 @@
 
 def as_bf16(mask):
     return jnp.where(mask, 1.0, 0.0).astype(jnp.bfloat16)
+
+
+def chunks_of(share, tile_rows):
+    size = share // PARTS
+    return [(y, i * size, size) for y in range(0, tile_rows, SUB) for i in range(PARTS)]
 
 
 def kernel(
@@ -85,14 +91,14 @@
         peers = peers + jnp.where(exists, 1, 0)
     pl.semaphore_wait(barrier, peers)
 
-    half = tile_cols // 2
-    chunks = [(y, x) for y in range(0, tile_rows, SUB) for x in range(0, tile_cols, half)]
+    chunks = chunks_of(share, tile_rows)
 
     def bulk(s, c):
-        y, x = chunks[c]
+        y, first, size = chunks[c]
+        part = pl.ds(first, size)
         return pltpu.make_async_remote_copy(
-            src_ref=phase.at[:, targets[s], pl.ds(y, SUB), pl.ds(x, half)],
-            dst_ref=stack.at[s, :, pl.ds(y, SUB), pl.ds(x, half)],
+            src_ref=phase.at[part, targets[s], pl.ds(y, SUB), :],
+            dst_ref=stack.at[s, part, pl.ds(y, SUB), :],
             send_sem=bulk_send.at[s - 1, c],
             recv_sem=bulk_recv.at[s - 1, c],
             device_id={"grp": targets[s]},
@@ -220,17 +226,18 @@
             jnp.bfloat16
         )
 
-    def series(c):
-        y, x = chunks[c]
-        for copy in bulks[c]:
-            copy.wait_recv()
-        data = stack[:, :, pl.ds(y, SUB), pl.ds(x, half)].reshape(full, half)
-        out = dot(weights[...], data).reshape(epochs, SUB, half)
-        disp[:, pl.ds(y, SUB), pl.ds(x, half)] = out.astype(jnp.bfloat16)
-        write(
-            disp.at[:, pl.ds(y, SUB), pl.ds(x, half)],
-            disp_hbm.at[:, pl.ds(y, SUB), pl.ds(x, half)],
-        )
+    def series(group):
+        for c in range(group * PARTS, (group + 1) * PARTS):
+            for copy in bulks[c]:
+                copy.wait_recv()
+        rows = pl.ds(group * SUB, SUB)
+        width = tile_cols // 2
+        for x in range(0, tile_cols, width):
+            cols = pl.ds(x, width)
+            data = stack[:, :, rows, cols].reshape(full, width)
+            out = dot(weights[...], data).reshape(epochs, SUB, width)
+            disp[:, rows, cols] = out.astype(jnp.bfloat16)
+            write(disp.at[:, rows, cols], disp_hbm.at[:, rows, cols])
 
     writes = []
 
@@ -238,8 +245,9 @@
         writes.append(pltpu.make_async_copy(source, target, out_sem.at[len(writes)]))
         writes[-1].start()
 
-    for c in range(EARLY):
-        series(c)
+    groups = tile_rows // SUB
+    for group in range(groups - 1):
+        series(group)
 
     for d in range(4):
         pl.when(there[d])(halos[d].wait_send)
@@ -268,8 +276,7 @@
     write(grad_rows, grad_rows_hbm)
     write(grad_cols, grad_cols_hbm)
 
-    for c in range(EARLY, len(chunks)):
-        series(c)
+    series(groups - 1)
     for c in range(len(chunks)):
         for copy in bulks[c]:
             copy.wait_send()
@@ -305,7 +312,7 @@
     hbm = pl.BlockSpec(memory_space=pltpu.HBM)
     f32, bf16 = jnp.float32, jnp.bfloat16
     others = n_grp - 1
-    chunks = (tile_rows // SUB) * 2
+    chunks = len(chunks_of(share, tile_rows))
     dma = pltpu.SemaphoreType.DMA
     results = pl.pallas_call(
         functools.partial(kernel, sizes),
@@ -340,7 +347,7 @@
             dma((others,)),
             dma((4,)),
             dma((4,)),
-            dma((chunks + 2,)),
+            dma((2 * (tile_rows // SUB) + 2,)),
         ],
         compiler_params=pltpu.CompilerParams(
             collective_id=0, has_side_effects=True, vmem_limit_bytes=GRANT

time: 35 us -> 36.1 us (1.031); the launches traced: 34.5 us -> 36 us
  Pallas kernels: 33.8 us -> 35.3 us
    pallas_call x1, Pallas kernels: 31.6 us -> 32.9 us  [on_device(): pl.pallas_call(functools.partial(kernel, sizes), out_shape=(jax.ShapeDtyp...]
where the time goes in v5:
time: 36.1 us; the launch traced here: 36 us
  Pallas kernels  35.3 us (98%)
  between operations  0.64 us (2%)
    pallas_call x1, Pallas kernels, on_device(): pl.pallas_call(functools.partial(kernel, sizes), out_shape=(jax.ShapeDtyp...  32.9 us
    pallas_call x1, Pallas kernels, on_device(): pl.pallas_call(write_out, out_shape=tuple((jax.ShapeDtypeStruct(r.shape,...  2.4 us

profile of v5, /device:TPU:0, one launch (start us, length us, event | category | flops | bytes accessed | tf_op | source)
XLA Modules:
  0.0 36.0 jit_solution(8849957239886139677)
XLA Ops:
  0.6 32.9 %shard_map.76 = (bf16[48,32,512]{2,1,0:T(8,128)(2,1)}, f32[32,512]{1,0:T(8,128)}, f32[32,512]{1,0:T(8,128)}) custom-call(bf16[32,2,32,512]{3,2,1,0:T(8,128)(2,1)} %phase.1, bf16[48,64]{1,0:T(8,128)(2,1)} %inverse_hbm.1, f32[4,3]{1,0:T(4,128)} %rotation_hbm.1, s32[32,512]{1,0:T(8,128)} %plate_hbm.1, s32[32,512]{1,0:T(8,128)} %coherent_hbm.1), custom_call_target="tpu_custom_call" | custom-call | flops 1610612736 | bytes 8388608 | tf_op jit(solution)/shard_map/pallas_call | solution.py:317
  33.6 2.4 %shard_map.77 = (bf16[48,32,512]{2,1,0:T(8,128)(2,1)}, f32[32,512]{1,0:T(8,128)}, f32[32,512]{1,0:T(8,128)}) custom-call(bf16[48,32,512]{2,1,0:T(8,128)(2,1)} %get-tuple-element.6.disp, f32[32,512]{1,0:T(8,128)} %get-tuple-element.7.grad_rows, f32[32,512]{1,0:T(8,128)} %get-tuple-element.8.grad_cols), custom_call_target="tpu_custom_call" | custom-call | tf_op jit(solution)/shard_map/pallas_call | solution.py:361

commit v6 on v4

--- a/solution.py
+++ b/solution.py
@@ -47,7 +47,7 @@
     sizes, phase, inverse_hbm, rotation_hbm, plate_hbm, coherent_hbm,
     disp_hbm, grad_rows_hbm, grad_cols_hbm,
     disp, grad_rows, grad_cols, stack, mine, inverse, rotation, plate, coherent, weights, partial, incoming, tall, wide,
-    local_sem, bulk_send, bulk_recv, rate_send, rate_recv, halo_send, halo_recv, out_sem,
+    local_sem, bulk_send, bulk_recv, rate_send, rate_recv, halo_send, halo_recv, out_sem, base,
 ):
     n_grp, n_row, n_col = sizes
     _, share, tile_rows, tile_cols = stack.shape
@@ -226,12 +226,17 @@
             jnp.bfloat16
         )
 
+    for y, x, width in chunks:
+        data = stack[0, :, pl.ds(y, SUB), pl.ds(x, width)].reshape(depth, width)
+        base[:, pl.ds(y // SUB * tile_cols + x, width)] = dot(weights[:, :depth], data)
+
     def series(c):
         y, x, width = chunks[c]
         for copy in bulks[c]:
             copy.wait_recv()
-        data = stack[:, :, pl.ds(y, SUB), pl.ds(x, width)].reshape(full, width)
-        out = dot(weights[...], data).reshape(epochs, SUB, width)
+        data = stack[1:, :, pl.ds(y, SUB), pl.ds(x, width)].reshape(full - depth, width)
+        out = base[:, pl.ds(y // SUB * tile_cols + x, width)] + dot(weights[:, depth:], data)
+        out = out.reshape(epochs, SUB, width)
         disp[:, pl.ds(y, SUB), pl.ds(x, width)] = out.astype(jnp.bfloat16)
         write(
             disp.at[:, pl.ds(y, SUB), pl.ds(x, width)],
@@ -347,6 +352,7 @@
             dma((4,)),
             dma((4,)),
             dma((chunks + 2,)),
+            pltpu.VMEM((epochs * SUB, tile_rows // SUB * tile_cols), f32),
         ],
         compiler_params=pltpu.CompilerParams(
             collective_id=0, has_side_effects=True, vmem_limit_bytes=GRANT

time: 35.1 us -> 34.7 us (0.989)
  Pallas kernels: 34.3 us -> 33.9 us
    pallas_call x1, Pallas kernels: 31.9 us -> 31.5 us  [on_device(): pl.pallas_call(functools.partial(kernel, sizes), out_shape=(jax.ShapeDtyp...]
where the time goes in v6:
time: 34.7 us; the launch traced here: 34.5 us
  Pallas kernels  33.9 us (98%)
  between operations  0.64 us (2%)
    pallas_call x1, Pallas kernels, on_device(): pl.pallas_call(functools.partial(kernel, sizes), out_shape=(jax.ShapeDtyp...  31.5 us
    pallas_call x1, Pallas kernels, on_device(): pl.pallas_call(write_out, out_shape=tuple((jax.ShapeDtypeStruct(r.shape,...  2.4 us

profile of v6, /device:TPU:0, one launch (start us, length us, event | category | flops | bytes accessed | tf_op | source)
XLA Modules:
  0.0 34.5 jit_solution(4497056450665320209)
XLA Ops:
  0.6 31.5 %shard_map.76 = (bf16[48,32,512]{2,1,0:T(8,128)(2,1)}, f32[32,512]{1,0:T(8,128)}, f32[32,512]{1,0:T(8,128)}) custom-call(bf16[32,2,32,512]{3,2,1,0:T(8,128)(2,1)} %phase.1, bf16[48,64]{1,0:T(8,128)(2,1)} %inverse_hbm.1, f32[4,3]{1,0:T(4,128)} %rotation_hbm.1, s32[32,512]{1,0:T(8,128)} %plate_hbm.1, s32[32,512]{1,0:T(8,128)} %coherent_hbm.1), custom_call_target="tpu_custom_call" | custom-call | flops 1610612736 | bytes 8388608 | tf_op jit(solution)/shard_map/pallas_call | solution.py:321
  32.1 2.4 %shard_map.77 = (bf16[48,32,512]{2,1,0:T(8,128)(2,1)}, f32[32,512]{1,0:T(8,128)}, f32[32,512]{1,0:T(8,128)}) custom-call(bf16[48,32,512]{2,1,0:T(8,128)(2,1)} %get-tuple-element.6.disp, f32[32,512]{1,0:T(8,128)} %get-tuple-element.7.grad_rows, f32[32,512]{1,0:T(8,128)} %get-tuple-element.8.grad_cols), custom_call_target="tpu_custom_call" | custom-call | tf_op jit(solution)/shard_map/pallas_call | solution.py:366
